TPU v7x, 512 devices: a whole 4x4x16 slice. The times are simulated.
512 devices in a mesh: dp: 16 (over x, y_lo, core), mp: 32 (over y_hi, z).
Axes of the slice: x: 4, y: 4 (y_hi: 2, y_lo: 2; y = y_hi * 2 + y_lo), z: 16, core: 2. Of those that a mesh axis runs over, the one named last changes fastest.
Arguments:
- field: bfloat16 [16, 32, 256, 2048], P('dp', None, 'mp'), may hold values from -6 to 6
- spec_weight: bfloat16 [32, 256, 2, 32, 32], P('dp', 'mp'), may hold values from -3 to 3
- skip_weight: bfloat16 [32, 32], replicated, may hold values from -1 to 1
- skip_bias: float32 [32], replicated, may hold values from -3 to 3
- out_grad: bfloat16 [16, 32, 256, 2048], P('dp', None, 'mp'), may hold values from -6 to 6
Outputs:
- activated: bfloat16 [16, 32, 256, 2048], P('dp', None, 'mp')
- field_grad: bfloat16 [16, 32, 256, 2048], P('dp', None, 'mp')
- weight_grad: float32 [32, 256, 2, 32, 32], P('dp', 'mp')
All inputs are finite; a program needn't handle non-finite values.
Results may differ from a plain program's by a relative error of at most 0.025.
Values may be sent and summed in bfloat16 or wider, within the bound.
A program may use at most 64 MiB of HBM per device.

v0:
```python
import math

import jax
import jax.numpy as jnp
import numpy as np
from jax import lax
from jax.experimental import pallas as pl
from jax.experimental.pallas import tpu as pltpu
from jax.sharding import PartitionSpec as P
from ml_dtypes import bfloat16 as np_bf16

C = 32
NX = 256
NY = 128
NZ = 16
KX = 32
KY = 32
KZ = 8
CELLS = NY * NZ
SLABS = 32
ROWS = NX // SLABS
PAIRS = KY * KZ // SLABS
GROUPS = 16
MODES = KX * PAIRS
LANES = C * ROWS
COEFS = 2 * KY * KZ
PIECE = 2 * PAIRS
SHARE = MODES // GROUPS
MIX = C * C
CHUNK = 512
MESH = pl.DeviceIdType.MESH
F32 = jnp.float32
BF16 = jnp.bfloat16


def grid_table():
    coef = np.arange(COEFS)
    owner, part, pair = coef // PIECE, coef // PAIRS % 2, coef % PAIRS
    mode = owner * PAIRS + pair
    y_freq = mode // KZ
    y_freq = np.where(y_freq < KY // 2, y_freq, y_freq - KY)
    z_freq = mode % KZ
    cell = np.arange(CELLS)
    phase = np.mod(y_freq[:, None] * (cell // NZ) * NZ + z_freq[:, None] * (cell % NZ) * NY, CELLS)
    angle = phase * (2.0 * math.pi / CELLS)
    return np.where(part[:, None] == 0, np.cos(angle), -np.sin(angle)).astype(np_bf16)


def slab_table():
    out = np.arange(2 * MODES)
    q, j, pair_out = out // MODES, out // PAIRS % KX, out % PAIRS
    src = np.arange(COEFS)
    slab, p, pair_in = src // PIECE, src // PAIRS % 2, src % PAIRS
    freq = np.where(j < KX // 2, j, j - KX)
    angle = np.mod(freq[:, None] * slab, SLABS) * (2.0 * math.pi / SLABS)
    sign = np.where(p[None, :] == q[:, None], 0.0, np.where(q[:, None] == 1, -1.0, 1.0))
    value = np.where(p[None, :] == q[:, None], np.cos(angle), sign * np.sin(angle))
    return np.where(pair_out[:, None] == pair_in, value, 0.0).astype(np_bf16)


def row_tables():
    j = np.arange(MODES) // PAIRS
    freq = np.where(j < KX // 2, j, j - KX)
    angle = freq[:, None] * (np.arange(LANES) % ROWS) * (2.0 * math.pi / NX)
    scale = 1.0 / math.sqrt(NX * NY * NZ)
    return np.stack([np.cos(angle) * scale, np.sin(angle) * scale]).astype(np.float32)


def spread_tables():
    half = LANES // 2
    by_in = (np.arange(half)[:, None] // ROWS == np.arange(half * C // ROWS) // C).astype(np_bf16)
    by_out = (np.arange(128)[:, None] % C == np.arange(LANES) // ROWS).astype(np_bf16)
    return by_in, by_in.T.copy(), by_out, by_out.T.copy()


def dot(a, b, dims=((1,), (0,))):
    return lax.dot_general(a, b, (dims, ((), ())), preferred_element_type=F32)


NT = ((1,), (1,))


def kernel(
    field_hbm, cot_hbm, weight_hbm, skip_ref, bias_ref,
    grid_hbm, slab_hbm, back_hbm, row_hbm, e_in_hbm, e_in_t_hbm, e_out_hbm, e_out_t_hbm,
    act_hbm, fgrad_hbm, wgrad_ref,
    field, cot, grid, slab, slab_b, rowt, e_in, e_in_t, e_out, e_out_t,
    act, gpre, fgrad, lin, weight, u_rep, coef, gs, wg, wg_recv, acc, send, recv, mixk, mixk_t,
    load_sem, store_sem, send_sem, recv_sem, gather_sem, reduce_sem,
):
    dp = lax.axis_index("dp")
    mp = lax.axis_index("mp")

    loads = [
        pltpu.make_async_copy(src, dst, load_sem.at[i])
        for i, (src, dst) in enumerate(
            [
                (field_hbm, field), (grid_hbm, grid), (slab_hbm, slab), (row_hbm, rowt),
                (e_in_hbm, e_in), (e_out_hbm, e_out), (back_hbm, slab_b), (cot_hbm, cot),
                (e_in_t_hbm, e_in_t), (e_out_t_hbm, e_out_t),
            ]
        )
    ]
    own_weight = pltpu.make_async_copy(
        weight_hbm, weight.at[pl.ds(pl.multiple_of(dp * SHARE, SHARE), SHARE)], load_sem.at[10]
    )
    for copy in loads:
        copy.start()
    own_weight.start()

    barrier = pltpu.get_barrier_semaphore()

    def greet_mp(i, carry):
        peer = lax.rem(mp + i, SLABS)
        pl.semaphore_signal(barrier, inc=1, device_id={"mp": peer}, device_id_type=MESH)
        return carry

    def greet_dp(i, carry):
        peer = lax.rem(dp + i, GROUPS)
        pl.semaphore_signal(barrier, inc=1, device_id={"dp": peer}, device_id_type=MESH)
        return carry

    lax.fori_loop(1, SLABS, greet_mp, 0)
    lax.fori_loop(1, GROUPS, greet_dp, 0)

    def exchange(phase):
        mine = pl.ds(pl.multiple_of(mp * PIECE, PIECE), PIECE)

        def push(i, carry):
            turn = SLABS - i
            hop = turn // 2
            shift = (hop + 1) // 2 * (2 * lax.rem(hop, 2) - 1)
            z = lax.rem(mp + shift + SLABS, SLABS // 2)
            y = lax.rem(mp // (SLABS // 2) + turn, 2)
            peer = y * (SLABS // 2) + z
            pltpu.make_async_remote_copy(
                src_ref=send.at[phase, pl.ds(pl.multiple_of(peer * PIECE, PIECE), PIECE)],
                dst_ref=recv.at[phase, mine],
                send_sem=send_sem.at[phase],
                recv_sem=recv_sem.at[phase],
                device_id={"mp": peer},
                device_id_type=MESH,
            ).start()
            return carry

        lax.fori_loop(1, SLABS, push, 0)
        recv[phase, mine, :] = send[phase, mine, :]

    def arrived(phase):
        block = recv.at[phase, pl.ds(0, COEFS - PIECE)]
        pltpu.make_async_copy(block, block, recv_sem.at[phase]).wait()

    loads[0].wait()
    loads[1].wait()
    send[0] = dot(grid[...], field[...], NT).astype(BF16)
    pl.semaphore_wait(barrier, SLABS + GROUPS - 2)
    exchange(0)

    def push_weight(i, carry):
        peer = lax.rem(dp + i, GROUPS)
        pltpu.make_async_remote_copy(
            src_ref=weight_hbm,
            dst_ref=weight.at[pl.ds(pl.multiple_of(dp * SHARE, SHARE), SHARE)],
            send_sem=gather_sem.at[0],
            recv_sem=gather_sem.at[1],
            device_id={"dp": peer},
            device_id_type=MESH,
        ).start()
        return carry

    lax.fori_loop(1, GROUPS, push_weight, 0)

    rep = (
        lax.broadcasted_iota(jnp.int32, (LANES, C), 0) // ROWS
        == lax.broadcasted_iota(jnp.int32, (LANES, C), 1)
    ).astype(F32)
    rep_b = rep.astype(BF16)
    same_row = (
        lax.broadcasted_iota(jnp.int32, (LANES, LANES), 0) % ROWS
        == lax.broadcasted_iota(jnp.int32, (LANES, LANES), 1) % ROWS
    )
    skip = skip_ref[...]
    by_out = dot(dot(rep_b, skip, NT).astype(BF16), rep_b, NT)
    by_in = dot(dot(rep_b, skip).astype(BF16), rep_b, NT)
    mixk[...] = jnp.where(same_row, by_out, 0.0).astype(BF16)
    mixk_t[...] = jnp.where(same_row, by_in, 0.0).astype(BF16)
    bias = jnp.sum(rep * bias_ref[...], axis=1, keepdims=True)

    def linear(i, carry):
        cells = pl.ds(pl.multiple_of(i * CHUNK, CHUNK), CHUNK)
        lin[:, cells] = dot(mixk[...], field[:, cells]) + bias
        return carry

    lax.fori_loop(0, CELLS // CHUNK, linear, 0)
    for copy in loads[2:]:
        copy.wait()
    own_weight.wait()

    double = jnp.where(
        lax.broadcasted_iota(jnp.int32, (MODES, LANES), 0) % PAIRS == 0, 1.0, 2.0
    )

    def to_modes(phase, factor):
        acc[...] = dot(slab[...], recv[phase])
        real, imag = acc[:MODES], acc[MODES:]
        cosine, sine = rowt[0], rowt[1]
        if factor is not None:
            cosine, sine = cosine * factor, sine * factor
        coef[0] = (real * cosine + imag * sine).astype(BF16)
        coef[1] = (imag * cosine - real * sine).astype(BF16)

    def from_modes(phase, real, imag, factor):
        cosine, sine = rowt[0], rowt[1]
        if factor is not None:
            cosine, sine = cosine * factor, sine * factor
        coef[0] = (real * cosine - imag * sine).astype(BF16)
        coef[1] = (imag * cosine + real * sine).astype(BF16)
        out = dot(slab_b[:, :MODES], coef[0]) + dot(slab_b[:, MODES:], coef[1])
        send[phase] = out.astype(BF16)

    arrived(0)
    to_modes(0, None)
    for q in range(2):
        for h in range(2):
            u_rep[q, :, h * CHUNK : (h + 1) * CHUNK] = dot(
                coef[q, :, h * 128 : (h + 1) * 128], e_in[...]
            )
    gathered = weight.at[pl.ds(0, MODES - SHARE)]
    pltpu.make_async_copy(gathered, gathered, gather_sem.at[1]).wait()

    STRIP = 32

    def mix(i, carry):
        rows = pl.ds(pl.multiple_of(i * STRIP, STRIP), STRIP)
        real = jnp.zeros((STRIP, 128), F32)
        imag = jnp.zeros((STRIP, 128), F32)
        for t in range(0, MIX, 128):
            u0 = u_rep[0, rows, t : t + 128]
            u1 = u_rep[1, rows, t : t + 128]
            w0 = weight[rows, t : t + 128].astype(F32)
            w1 = weight[rows, MIX + t : MIX + t + 128].astype(F32)
            real = real + (u0 * w0 - u1 * w1)
            imag = imag + (u0 * w1 + u1 * w0)
        gs[0, rows, :128] = real.astype(BF16)
        gs[1, rows, :128] = imag.astype(BF16)
        return carry

    lax.fori_loop(0, MODES // STRIP, mix, 0)
    from_modes(1, dot(gs[0, :, :128], e_out[...]), dot(gs[1, :, :128], e_out[...]), double)
    exchange(1)
    arrived(1)

    back = recv[1].T
    acc[...] = jnp.zeros((COEFS, LANES), F32)
    root = math.sqrt(2.0 / math.pi)
    cube = 0.044715

    def activate(i, carry):
        cells = pl.ds(pl.multiple_of(i * CHUNK, CHUNK), CHUNK)
        pre = dot(back, grid[:, cells]) + lin[:, cells]
        square = pre * pre
        bent = jnp.tanh(pre * (root + (root * cube) * square))
        half = 0.5 * pre
        upper = 0.5 + 0.5 * bent
        act[:, cells] = (pre * upper).astype(BF16)
        slope = upper + half * (1.0 - bent * bent) * (root + (3.0 * root * cube) * square)
        grad = (cot[:, cells].astype(F32) * slope).astype(BF16)
        gpre[:, cells] = grad
        acc[...] += dot(grid[:, cells], grad, NT)
        return carry

    lax.fori_loop(0, CELLS // CHUNK, activate, 0)
    send[2] = acc[...].astype(BF16)
    exchange(2)
    store_act = pltpu.make_async_copy(act, act_hbm, store_sem.at[0])
    store_act.start()

    def linear_back(i, carry):
        cells = pl.ds(pl.multiple_of(i * CHUNK, CHUNK), CHUNK)
        lin[:, cells] = dot(mixk_t[...], gpre[:, cells])
        return carry

    lax.fori_loop(0, CELLS // CHUNK, linear_back, 0)
    arrived(2)
    to_modes(2, double)
    g_real = dot(coef[0], e_out_t[...])
    g_imag = dot(coef[1], e_out_t[...])
    acc[:MODES, :128] = g_real
    acc[MODES:, :128] = g_imag

    def mix_back(i, carry):
        rows = pl.ds(pl.multiple_of(i * STRIP, STRIP), STRIP)
        rows_imag = pl.ds(pl.multiple_of(i * STRIP + MODES, STRIP), STRIP)
        g0 = acc[rows, :128]
        g1 = acc[rows_imag, :128]
        for t in range(0, MIX, 128):
            w0 = weight[rows, t : t + 128].astype(F32)
            w1 = weight[rows, MIX + t : MIX + t + 128].astype(F32)
            gs[0, rows, t : t + 128] = (w0 * g0 + w1 * g1).astype(BF16)
            gs[1, rows, t : t + 128] = (w0 * g1 - w1 * g0).astype(BF16)
        return carry

    lax.fori_loop(0, MODES // STRIP, mix_back, 0)

    def fold(q):
        return jnp.concatenate(
            [dot(gs[q, :, :CHUNK], e_in_t[...]), dot(gs[q, :, CHUNK:], e_in_t[...])], axis=1
        )

    from_modes(3, fold(0), fold(1), None)
    exchange(3)

    def outer(i, carry):
        rows = pl.ds(pl.multiple_of(i * STRIP, STRIP), STRIP)
        rows_imag = pl.ds(pl.multiple_of(i * STRIP + MODES, STRIP), STRIP)
        g0 = acc[rows, :128]
        g1 = acc[rows_imag, :128]
        for t in range(0, MIX, 128):
            u0 = u_rep[0, rows, t : t + 128]
            u1 = u_rep[1, rows, t : t + 128]
            wg[rows, t : t + 128] = (u0 * g0 + u1 * g1).astype(BF16)
            wg[rows, MIX + t : MIX + t + 128] = (u0 * g1 - u1 * g0).astype(BF16)
        return carry

    lax.fori_loop(0, MODES // STRIP, outer, 0)

    def push_grad(i, carry):
        peer = lax.rem(dp + i, GROUPS)
        pltpu.make_async_remote_copy(
            src_ref=wg.at[pl.ds(pl.multiple_of(peer * SHARE, SHARE), SHARE)],
            dst_ref=wg_recv.at[pl.ds(pl.multiple_of(dp * SHARE, SHARE), SHARE)],
            send_sem=reduce_sem.at[0],
            recv_sem=reduce_sem.at[1],
            device_id={"dp": peer},
            device_id_type=MESH,
        ).start()
        return carry

    lax.fori_loop(1, GROUPS, push_grad, 0)
    own = pl.ds(pl.multiple_of(dp * SHARE, SHARE), SHARE)
    wg_recv[own, :] = wg[own, :]

    arrived(3)
    grad_back = recv[3].T

    def finish(i, carry):
        cells = pl.ds(pl.multiple_of(i * CHUNK, CHUNK), CHUNK)
        fgrad[:, cells] = (dot(grad_back, grid[:, cells]) + lin[:, cells]).astype(BF16)
        return carry

    lax.fori_loop(0, CELLS // CHUNK, finish, 0)
    store_grad = pltpu.make_async_copy(fgrad, fgrad_hbm, store_sem.at[1])
    store_grad.start()

    reduced = wg_recv.at[pl.ds(0, MODES - SHARE)]
    pltpu.make_async_copy(reduced, reduced, reduce_sem.at[1]).wait()
    for t in range(0, 2 * MIX, 256):
        total = wg_recv[0:SHARE, t : t + 256].astype(F32)
        for s in range(1, GROUPS):
            total = total + wg_recv[s * SHARE : (s + 1) * SHARE, t : t + 256].astype(F32)
        wgrad_ref[:, t : t + 256] = total

    for phase in range(4):
        block = send.at[phase, pl.ds(0, COEFS - PIECE)]
        pltpu.make_async_copy(block, block, send_sem.at[phase]).wait()
    pltpu.make_async_copy(gathered, gathered, gather_sem.at[0]).wait()
    sent = wg.at[pl.ds(0, MODES - SHARE)]
    pltpu.make_async_copy(sent, sent, reduce_sem.at[0]).wait()
    store_act.wait()
    store_grad.wait()


def body(field, spec_weight, skip_weight, skip_bias, out_grad):
    slab = slab_table()
    by_in, by_in_t, by_out, by_out_t = spread_tables()
    tables = [
        jnp.asarray(t)
        for t in (grid_table(), slab, slab.T.copy(), row_tables(), by_in, by_in_t, by_out, by_out_t)
    ]
    anywhere = pl.BlockSpec(memory_space=pl.ANY)
    vmem = pl.BlockSpec(memory_space=pltpu.VMEM)
    scratch = [
        pltpu.VMEM((LANES, CELLS), BF16),
        pltpu.VMEM((LANES, CELLS), BF16),
        pltpu.VMEM((COEFS, CELLS), BF16),
        pltpu.VMEM((2 * MODES, COEFS), BF16),
        pltpu.VMEM((COEFS, 2 * MODES), BF16),
        pltpu.VMEM((2, MODES, LANES), F32),
        pltpu.VMEM(by_in.shape, BF16),
        pltpu.VMEM(by_in_t.shape, BF16),
        pltpu.VMEM(by_out.shape, BF16),
        pltpu.VMEM(by_out_t.shape, BF16),
        pltpu.VMEM((LANES, CELLS), BF16),
        pltpu.VMEM((LANES, CELLS), BF16),
        pltpu.VMEM((LANES, CELLS), BF16),
        pltpu.VMEM((LANES, CELLS), F32),
        pltpu.VMEM((MODES, 2 * MIX), BF16),
        pltpu.VMEM((2, MODES, MIX), F32),
        pltpu.VMEM((2, MODES, LANES), BF16),
        pltpu.VMEM((2, MODES, MIX), BF16),
        pltpu.VMEM((MODES, 2 * MIX), BF16),
        pltpu.VMEM((MODES, 2 * MIX), BF16),
        pltpu.VMEM((COEFS, LANES), F32),
        pltpu.VMEM((4, COEFS, LANES), BF16),
        pltpu.VMEM((4, COEFS, LANES), BF16),
        pltpu.VMEM((LANES, LANES), BF16),
        pltpu.VMEM((LANES, LANES), BF16),
        pltpu.SemaphoreType.DMA((11,)),
        pltpu.SemaphoreType.DMA((2,)),
        pltpu.SemaphoreType.DMA((4,)),
        pltpu.SemaphoreType.DMA((4,)),
        pltpu.SemaphoreType.DMA((2,)),
        pltpu.SemaphoreType.DMA((2,)),
    ]
    act, fgrad, wgrad = pl.pallas_call(
        kernel,
        out_shape=(
            jax.ShapeDtypeStruct((LANES, CELLS), BF16),
            jax.ShapeDtypeStruct((LANES, CELLS), BF16),
            jax.ShapeDtypeStruct((SHARE, 2 * MIX), F32),
        ),
        in_specs=[anywhere] * 3 + [vmem] * 2 + [anywhere] * 8,
        out_specs=(anywhere, anywhere, vmem),
        scratch_shapes=scratch,
        compiler_params=pltpu.CompilerParams(
            collective_id=0, has_side_effects=True, vmem_limit_bytes=48 * 1024 * 1024
        ),
        cost_estimate=pl.CostEstimate(
            flops=3_600_000_000, bytes_accessed=10_000_000, transcendentals=524288
        ),
        name="fourier_layer",
    )(
        field.reshape(LANES, CELLS), out_grad.reshape(LANES, CELLS),
        spec_weight.reshape(SHARE, 2 * MIX), skip_weight, skip_bias.reshape(1, C), *tables,
    )
    return (
        act.reshape(field.shape), fgrad.reshape(field.shape), wgrad.reshape(spec_weight.shape)
    )


def solution(mesh):
    in_specs = (
        P("dp", None, "mp", None),
        P("dp", "mp", None, None, None),
        P(),
        P(),
        P("dp", None, "mp", None),
    )
    out_specs = (
        P("dp", None, "mp", None),
        P("dp", None, "mp", None),
        P("dp", "mp", None, None, None),
    )
    return jax.shard_map(body, mesh=mesh, in_specs=in_specs, out_specs=out_specs, check_vma=False)
```

profile of v0, /device:TPU:1, one launch (start us, length us, event | category | flops | bytes accessed | tf_op | source)
XLA Modules:
  0.0 102.3 jit_solution(5931786776804607513)
XLA Ops:
  0.6 1.2 %reshape.29.weight_hbm = bf16[16,2048]{1,0:T(8,128)(2,1)S(1)} reshape(bf16[2,8,2,32,32]{4,3,2,1,0:T(8,128)(2,1)} %param.14) | data formatting | bytes 131072 | tf_op jit(solution)/shard_map/reshape | solution.py:434
  1.9 0.0 copy-start
  1.9 1.2 %copy-done = bf16[1,32,8,2048]{3,2,1,0:T(8,128)(2,1)S(1)} copy-done((bf16[1,32,8,2048]{3,2,1,0:T(8,128)(2,1)S(1)}, bf16[1,32,8,2048]{3,2,1,0:T(8,128)(2,1)}, u32[]{:S(2)}) %copy-start) | copy-done | bytes 1048600
  3.1 0.0 copy-start.1
  3.1 0.7 copy-done.1
  3.8 0.0 copy-start.2
  3.8 0.7 copy-done.2
  4.5 0.0 copy-start.3
  4.5 1.0 %copy-done.3 = f32[2,256,256]{2,1,0:T(8,128)S(1)} copy-done((f32[2,256,256]{2,1,0:T(8,128)S(1)}, f32[2,256,256]{2,1,0:T(8,128)}, u32[]{:S(2)}) %copy-start.3) | copy-done | bytes 524312
  5.5 0.0 copy-start.4
  5.5 1.0 %copy-done.4 = bf16[512,512]{1,0:T(8,128)(2,1)S(1)} copy-done((bf16[512,512]{1,0:T(8,128)(2,1)S(1)}, bf16[512,512]{1,0:T(8,128)(2,1)}, u32[]{:S(2)}) %copy-start.4) | copy-done | bytes 524312
  6.5 0.0 copy-start.5
  6.5 1.0 %copy-done.5 = bf16[512,512]{1,0:T(8,128)(2,1)S(1)} copy-done((bf16[512,512]{1,0:T(8,128)(2,1)S(1)}, bf16[512,512]{1,0:T(8,128)(2,1)}, u32[]{:S(2)}) %copy-start.5) | copy-done | bytes 524312
  7.6 0.0 copy-start.6
  7.6 0.9 copy-done.6
  8.5 0.0 copy-start.7
  8.5 0.9 copy-done.7
  9.4 0.0 copy-start.8
  9.4 0.8 copy-done.8
  10.2 0.0 copy-start.9
  10.2 0.8 copy-done.9
  11.1 88.3 %fourier_layer.1 = (bf16[256,2048]{1,0:T(8,128)(2,1)S(1)}, bf16[256,2048]{1,0:T(8,128)(2,1)S(1)}, f32[16,2048]{1,0:T(8,128)S(1)}) custom-call(bf16[256,2048]{1,0:T(8,128)(2,1)S(1)} %bitcast.9, bf16[256,2048]{1,0:T(8,128)(2,1)} %bitcast.11, bf16[16,2048]{1,0:T(8,128)(2,1)S(1)} %reshape.29.weight_hbm, bf16[32,32]{1,0:T(8,128)(2,1)S(1)} %copy-done.1, ...), custom_call_target="tpu_custom_call" | custom-call | flops 3600000000 | bytes 10000000 | tf_op jit(solution)/shard_map/fourier_layer/pallas_call | solution.py:415
  99.4 1.0 reshape.33
  100.4 1.0 copy.18
  101.3 1.0 copy.19
Async XLA Ops:
  1.9 1.2 %copy-start = (bf16[1,32,8,2048]{3,2,1,0:T(8,128)(2,1)S(1)}, bf16[1,32,8,2048]{3,2,1,0:T(8,128)(2,1)}, u32[]{:S(2)}) copy-start(bf16[1,32,8,2048]{3,2,1,0:T(8,128)(2,1)} %param.13) | copy-start | bytes 3145732
  3.1 0.7 copy-start.1
  3.8 0.7 copy-start.2
  4.5 1.0 %copy-start.3 = (f32[2,256,256]{2,1,0:T(8,128)S(1)}, f32[2,256,256]{2,1,0:T(8,128)}, u32[]{:S(2)}) copy-start(f32[2,256,256]{2,1,0:T(8,128)} %constant.19.clone.row_hbm) | copy-start | bytes 1572868
  5.5 1.0 %copy-start.4 = (bf16[512,512]{1,0:T(8,128)(2,1)S(1)}, bf16[512,512]{1,0:T(8,128)(2,1)}, u32[]{:S(2)}) copy-start(bf16[512,512]{1,0:T(8,128)(2,1)} %constant.18.clone.back_hbm) | copy-start | bytes 1572868
  6.5 1.0 %copy-start.5 = (bf16[512,512]{1,0:T(8,128)(2,1)S(1)}, bf16[512,512]{1,0:T(8,128)(2,1)}, u32[]{:S(2)}) copy-start(bf16[512,512]{1,0:T(8,128)(2,1)} %constant.17.clone.slab_hbm) | copy-start | bytes 1572868
  7.6 0.9 copy-start.6
  8.5 0.9 copy-start.7
  9.4 0.8 copy-start.8
  10.2 0.8 copy-start.9
where the time goes:
time: 103 us; the launch traced here: 102 us
  Pallas kernels  88.3 us (86%)
  local copies, waits for them, and re-layouts  13.3 us (13%)
    pallas_call x1, Pallas kernels, body(): pl.pallas_call(kernel, out_shape=(jax.ShapeDtypeStruct((LANES, CELLS), BF...  88.3 us
    unnamed x22, local copies, waits for them, and re-layouts  11.1 us

commit v1 on v0

v1 whole, which is shorter than its diff:
```python
import math

import jax
import jax.numpy as jnp
import numpy as np
from jax import lax
from jax.experimental import pallas as pl
from jax.experimental.pallas import tpu as pltpu
from jax.sharding import PartitionSpec as P
from ml_dtypes import bfloat16 as np_bf16

C = 32
NX = 256
NY = 128
NZ = 16
KX = 32
KY = 32
KZ = 8
CELLS = NY * NZ
SLABS = 32
ROWS = NX // SLABS
PAIRS = KY * KZ // SLABS
PARTS = 2
PART = PAIRS // PARTS
GROUPS = 16
OWN = KX // GROUPS
MODES = KX * PART
LANES = C * ROWS
COEFS = SLABS * 2 * PART
PIECE = 2 * PART
SHARE = OWN * PART
MIX = C * C
CHUNK = 512
STRIP = 32
MESH = pl.DeviceIdType.MESH
F32 = jnp.float32
BF16 = jnp.bfloat16


def grid_table():
    chunk, coef = np.arange(PARTS)[:, None], np.arange(COEFS)[None, :]
    owner, part, pair = coef // PIECE, coef // PART % 2, coef % PART
    mode = owner * PAIRS + chunk * PART + pair
    y_freq = mode // KZ
    y_freq = np.where(y_freq < KY // 2, y_freq, y_freq - KY)
    z_freq = mode % KZ
    cell = np.arange(CELLS)
    phase = np.mod(
        y_freq[..., None] * (cell // NZ) * NZ + z_freq[..., None] * (cell % NZ) * NY, CELLS
    )
    angle = phase * (2.0 * math.pi / CELLS)
    return np.where(part[..., None] == 0, np.cos(angle), -np.sin(angle)).astype(np_bf16)


def slab_table():
    out = np.arange(2 * MODES)
    q, j, pair_out = out // MODES, out // PART % KX, out % PART
    src = np.arange(COEFS)
    slab, p, pair_in = src // PIECE, src // PART % 2, src % PART
    freq = np.where(j < KX // 2, j, j - KX)
    angle = np.mod(freq[:, None] * slab, SLABS) * (2.0 * math.pi / SLABS)
    sign = np.where(q[:, None] == 1, -1.0, 1.0)
    value = np.where(p[None, :] == q[:, None], np.cos(angle), sign * np.sin(angle))
    return np.where(pair_out[:, None] == pair_in, value, 0.0).astype(np_bf16)


def row_tables():
    j = np.arange(MODES) // PART
    freq = np.where(j < KX // 2, j, j - KX)
    angle = freq[:, None] * (np.arange(LANES) % ROWS) * (2.0 * math.pi / NX)
    scale = 1.0 / math.sqrt(NX * NY * NZ)
    return np.stack([np.cos(angle) * scale, np.sin(angle) * scale]).astype(np.float32)


def spread_tables():
    half = LANES // 2
    by_in = (np.arange(half)[:, None] // ROWS == np.arange(half * C // ROWS) // C).astype(np_bf16)
    by_out = (np.arange(128)[:, None] % C == np.arange(LANES) // ROWS).astype(np_bf16)
    return by_in, by_in.T.copy(), by_out, by_out.T.copy()


def regroup(first, second):
    upper = lax.broadcasted_iota(jnp.int32, first.shape, 0) < PART
    return (
        jnp.where(upper, first, pltpu.roll(second, PART, 0)),
        jnp.where(upper, pltpu.roll(first, PART, 0), second),
    )


def dot(a, b, dims=((1,), (0,))):
    return lax.dot_general(a, b, (dims, ((), ())), preferred_element_type=F32)


NT = ((1,), (1,))


def kernel(
    field_hbm, cot_hbm, weight_hbm, skip_hbm, bias_hbm,
    grid_hbm, slab_hbm, back_hbm, row_hbm, e_in_hbm, e_in_t_hbm, e_out_hbm, e_out_t_hbm,
    act_hbm, fgrad_hbm, wgrad_ref,
    field, cot, skip_v, bias_v, grid, slab, slab_b, rowt, e_in, e_in_t, e_out, e_out_t,
    act, gpre, fgrad, lin, share, weight, u_rep, coef, gs, wg, wg_recv, acc, send, recv, mixk, mixk_t,
    load_sem, store_sem, send_sem, recv_sem, gather_sem, reduce_sem,
):
    dp = lax.axis_index("dp")
    mp = lax.axis_index("mp")

    loads = [
        pltpu.make_async_copy(src, dst, load_sem.at[i])
        for i, (src, dst) in enumerate(
            [
                (field_hbm, field), (grid_hbm.at[0], grid.at[0]), (grid_hbm.at[1], grid.at[1]),
                (skip_hbm, skip_v), (bias_hbm, bias_v), (slab_hbm, slab), (row_hbm, rowt),
                (e_in_hbm, e_in), (e_out_hbm, e_out), (back_hbm, slab_b), (cot_hbm, cot),
                (e_in_t_hbm, e_in_t), (e_out_t_hbm, e_out_t), (weight_hbm, share),
            ]
        )
    ]
    for copy in loads:
        copy.start()

    barrier = pltpu.get_barrier_semaphore()

    def greet_mp(i, carry):
        peer = lax.rem(mp + i, SLABS)
        pl.semaphore_signal(barrier, inc=1, device_id={"mp": peer}, device_id_type=MESH)
        return carry

    def greet_dp(i, carry):
        peer = lax.rem(dp + i, GROUPS)
        pl.semaphore_signal(barrier, inc=1, device_id={"dp": peer}, device_id_type=MESH)
        return carry

    lax.fori_loop(1, SLABS, greet_mp, 0)
    lax.fori_loop(1, GROUPS, greet_dp, 0)

    def exchange(phase, part):
        slot = phase * PARTS + part

        def push(i, carry):
            turn = SLABS - i
            hop = turn // 2
            shift = (hop + 1) // 2 * (2 * lax.rem(hop, 2) - 1)
            z = lax.rem(mp + shift + SLABS, SLABS // 2)
            y = lax.rem(mp // (SLABS // 2) + turn, 2)
            peer = y * (SLABS // 2) + z
            pltpu.make_async_remote_copy(
                src_ref=send.at[slot, peer],
                dst_ref=recv.at[slot, mp],
                send_sem=send_sem.at[slot],
                recv_sem=recv_sem.at[slot],
                device_id={"mp": peer},
                device_id_type=MESH,
            ).start()
            return carry

        lax.fori_loop(1, SLABS, push, 0)
        recv[slot, mp] = send[slot, mp]

    def arrived(phase, part):
        slot = phase * PARTS + part
        block = recv.at[slot, pl.ds(0, SLABS - 1)]
        pltpu.make_async_copy(block, block, recv_sem.at[slot]).wait()
        return recv[slot].reshape(COEFS, LANES)

    def outgoing(phase, part, value):
        send[phase * PARTS + part] = value.astype(BF16).reshape(SLABS, PIECE, LANES)

    def cells_of(i):
        return pl.ds(pl.multiple_of(i * CHUNK, CHUNK), CHUNK)

    loads[0].wait()
    loads[1].wait()
    outgoing(0, 0, dot(grid[0], field[...], NT))
    pl.semaphore_wait(barrier, SLABS + GROUPS - 2)
    exchange(0, 0)
    loads[2].wait()
    outgoing(0, 1, dot(grid[1], field[...], NT))
    exchange(0, 1)

    def push_weight(i, carry):
        peer = lax.rem(dp + i, GROUPS)
        pltpu.make_async_remote_copy(
            src_ref=weight.at[:, dp],
            dst_ref=weight.at[:, dp],
            send_sem=gather_sem.at[0],
            recv_sem=gather_sem.at[1],
            device_id={"dp": peer},
            device_id_type=MESH,
        ).start()
        return carry

    for copy in loads[3:]:
        copy.wait()
    parted = regroup(share[:SHARE].astype(F32), share[SHARE:].astype(F32))
    for part in range(PARTS):
        weight[part, dp] = parted[part].astype(BF16)
    lax.fori_loop(1, GROUPS, push_weight, 0)

    rep = (
        lax.broadcasted_iota(jnp.int32, (LANES, C), 0) // ROWS
        == lax.broadcasted_iota(jnp.int32, (LANES, C), 1)
    ).astype(F32)
    rep_b = rep.astype(BF16)
    same_row = (
        lax.broadcasted_iota(jnp.int32, (LANES, LANES), 0) % ROWS
        == lax.broadcasted_iota(jnp.int32, (LANES, LANES), 1) % ROWS
    )
    skip = skip_v[...]
    by_out = dot(dot(rep_b, skip, NT).astype(BF16), rep_b, NT)
    by_in = dot(dot(rep_b, skip).astype(BF16), rep_b, NT)
    mixk[...] = jnp.where(same_row, by_out, 0.0).astype(BF16)
    mixk_t[...] = jnp.where(same_row, by_in, 0.0).astype(BF16)
    bias = jnp.sum(rep * bias_v[...], axis=1, keepdims=True)

    def linear(i, carry):
        lin[:, cells_of(i)] = dot(mixk[...], field[:, cells_of(i)]) + bias
        return carry

    lax.fori_loop(0, CELLS // CHUNK, linear, 0)

    doubled = [
        jnp.where(
            lax.broadcasted_iota(jnp.int32, (MODES, LANES), 0) % PART == 0, 1.0, 2.0
        ),
        2.0,
    ]

    def to_modes(block, factor):
        both = dot(slab[...], block)
        real, imag = both[:MODES], both[MODES:]
        cosine, sine = rowt[0] * factor, rowt[1] * factor
        coef[0] = (real * cosine + imag * sine).astype(BF16)
        coef[1] = (imag * cosine - real * sine).astype(BF16)

    def from_modes(real, imag, factor):
        cosine, sine = rowt[0] * factor, rowt[1] * factor
        coef[0] = (real * cosine - imag * sine).astype(BF16)
        coef[1] = (imag * cosine + real * sine).astype(BF16)
        return dot(slab_b[:, :MODES], coef[0]) + dot(slab_b[:, MODES:], coef[1])

    def strip_of(i):
        return pl.ds(pl.multiple_of(i * STRIP, STRIP), STRIP)

    def weights_of(part, i, t):
        owners = pl.ds(i * (STRIP // SHARE), STRIP // SHARE)
        w0 = weight[part, owners, :, t : t + 128].astype(F32).reshape(STRIP, 128)
        w1 = weight[part, owners, :, MIX + t : MIX + t + 128].astype(F32).reshape(STRIP, 128)
        return w0, w1

    for part in range(PARTS):
        block = arrived(0, part)
        to_modes(block, 1.0)
        for q in range(2):
            for h in range(2):
                u_rep[part, q, :, h * MIX // 2 : (h + 1) * MIX // 2] = dot(
                    coef[q, :, h * 128 : (h + 1) * 128], e_in[...]
                )
        if part == 0:
            gathered = weight.at[:, pl.ds(0, GROUPS - 1)]
            pltpu.make_async_copy(gathered, gathered, gather_sem.at[1]).wait()

        def mix(i, carry):
            rows = strip_of(i)
            real = jnp.zeros((STRIP, 128), F32)
            imag = jnp.zeros((STRIP, 128), F32)
            for t in range(0, MIX, 128):
                u0 = u_rep[part, 0, rows, t : t + 128]
                u1 = u_rep[part, 1, rows, t : t + 128]
                w0, w1 = weights_of(part, i, t)
                real = real + (u0 * w0 - u1 * w1)
                imag = imag + (u0 * w1 + u1 * w0)
            gs[0, rows, :128] = real.astype(BF16)
            gs[1, rows, :128] = imag.astype(BF16)
            return carry

        lax.fori_loop(0, MODES // STRIP, mix, 0)
        outgoing(
            1,
            part,
            from_modes(
                dot(gs[0, :, :128], e_out[...]), dot(gs[1, :, :128], e_out[...]), doubled[part]
            ),
        )
        exchange(1, part)

    back = arrived(1, 0).T

    def spread(i, carry):
        lin[:, cells_of(i)] += dot(back, grid[0, :, cells_of(i)])
        return carry

    lax.fori_loop(0, CELLS // CHUNK, spread, 0)
    back_last = arrived(1, 1).T
    acc[...] = jnp.zeros((PARTS, COEFS, LANES), F32)
    root = math.sqrt(2.0 / math.pi)
    cube = 0.044715

    def activate(i, carry):
        cells = cells_of(i)
        pre = dot(back_last, grid[1, :, cells]) + lin[:, cells]
        square = pre * pre
        bent = jnp.tanh(pre * (root + (root * cube) * square))
        half = 0.5 * pre
        upper = 0.5 + 0.5 * bent
        act[:, cells] = (pre * upper).astype(BF16)
        slope = upper + half * (1.0 - bent * bent) * (root + (3.0 * root * cube) * square)
        grad = (cot[:, cells].astype(F32) * slope).astype(BF16)
        gpre[:, cells] = grad
        acc[0] += dot(grid[0, :, cells], grad, NT)
        acc[1] += dot(grid[1, :, cells], grad, NT)
        return carry

    lax.fori_loop(0, CELLS // CHUNK, activate, 0)
    for part in range(PARTS):
        outgoing(2, part, acc[part])
        exchange(2, part)
    store_act = pltpu.make_async_copy(act, act_hbm, store_sem.at[0])
    store_act.start()

    def linear_back(i, carry):
        lin[:, cells_of(i)] = dot(mixk_t[...], gpre[:, cells_of(i)])
        return carry

    lax.fori_loop(0, CELLS // CHUNK, linear_back, 0)

    for part in range(PARTS):
        to_modes(arrived(2, part), doubled[part])
        for q in range(2):
            acc[q, :MODES, :128] = dot(coef[q], e_out_t[...])

        def mix_back(i, carry):
            rows = strip_of(i)
            g0 = acc[0, rows, :128]
            g1 = acc[1, rows, :128]
            for t in range(0, MIX, 128):
                w0, w1 = weights_of(part, i, t)
                gs[0, rows, t : t + 128] = (w0 * g0 + w1 * g1).astype(BF16)
                gs[1, rows, t : t + 128] = (w0 * g1 - w1 * g0).astype(BF16)
            return carry

        lax.fori_loop(0, MODES // STRIP, mix_back, 0)

        def fold(q):
            halves = [dot(gs[q, :, h : h + MIX // 2], e_in_t[...]) for h in (0, MIX // 2)]
            return jnp.concatenate(halves, axis=1)

        outgoing(3, part, from_modes(fold(0), fold(1), 1.0))
        exchange(3, part)

        def outer(i, carry):
            rows = strip_of(i)
            owners = pl.ds(i * (STRIP // SHARE), STRIP // SHARE)
            g0 = acc[0, rows, :128]
            g1 = acc[1, rows, :128]
            for t in range(0, MIX, 128):
                u0 = u_rep[part, 0, rows, t : t + 128]
                u1 = u_rep[part, 1, rows, t : t + 128]
                real = (u0 * g0 + u1 * g1).astype(BF16)
                imag = (u0 * g1 - u1 * g0).astype(BF16)
                wg[part, owners, :, t : t + 128] = real.reshape(-1, SHARE, 128)
                wg[part, owners, :, MIX + t : MIX + t + 128] = imag.reshape(-1, SHARE, 128)
            return carry

        lax.fori_loop(0, MODES // STRIP, outer, 0)

        def push_grad(i, carry):
            peer = lax.rem(dp + i, GROUPS)
            pltpu.make_async_remote_copy(
                src_ref=wg.at[part, peer],
                dst_ref=wg_recv.at[part, dp],
                send_sem=reduce_sem.at[part],
                recv_sem=reduce_sem.at[PARTS + part],
                device_id={"dp": peer},
                device_id_type=MESH,
            ).start()
            return carry

        lax.fori_loop(1, GROUPS, push_grad, 0)
        wg_recv[part, dp] = wg[part, dp]

    grad_back = arrived(3, 0).T

    def spread_back(i, carry):
        lin[:, cells_of(i)] += dot(grad_back, grid[0, :, cells_of(i)])
        return carry

    lax.fori_loop(0, CELLS // CHUNK, spread_back, 0)
    grad_back_last = arrived(3, 1).T

    def finish(i, carry):
        cells = cells_of(i)
        fgrad[:, cells] = (dot(grad_back_last, grid[1, :, cells]) + lin[:, cells]).astype(BF16)
        return carry

    lax.fori_loop(0, CELLS // CHUNK, finish, 0)
    store_grad = pltpu.make_async_copy(fgrad, fgrad_hbm, store_sem.at[1])
    store_grad.start()

    totals = []
    for part in range(PARTS):
        reduced = wg_recv.at[part, pl.ds(0, GROUPS - 1)]
        pltpu.make_async_copy(reduced, reduced, reduce_sem.at[PARTS + part]).wait()
        total = wg_recv[part, 0].astype(F32)
        for s in range(1, GROUPS):
            total = total + wg_recv[part, s].astype(F32)
        totals.append(total)
    whole = regroup(*totals)
    for part in range(PARTS):
        wgrad_ref[part * SHARE : (part + 1) * SHARE] = whole[part]

    for slot in range(4 * PARTS):
        block = send.at[slot, pl.ds(0, SLABS - 1)]
        pltpu.make_async_copy(block, block, send_sem.at[slot]).wait()
    pltpu.make_async_copy(gathered, gathered, gather_sem.at[0]).wait()
    for part in range(PARTS):
        sent = wg.at[part, pl.ds(0, GROUPS - 1)]
        pltpu.make_async_copy(sent, sent, reduce_sem.at[part]).wait()
    store_act.wait()
    store_grad.wait()


def body(field, spec_weight, skip_weight, skip_bias, out_grad):
    slab = slab_table()
    by_in, by_in_t, by_out, by_out_t = spread_tables()
    tables = [
        jnp.asarray(t)
        for t in (grid_table(), slab, slab.T.copy(), row_tables(), by_in, by_in_t, by_out, by_out_t)
    ]
    anywhere = pl.BlockSpec(memory_space=pl.ANY)
    vmem = pl.BlockSpec(memory_space=pltpu.VMEM)
    scratch = [
        pltpu.VMEM((LANES, CELLS), BF16),
        pltpu.VMEM((LANES, CELLS), BF16),
        pltpu.VMEM((C, C), BF16),
        pltpu.VMEM((1, C), F32),
        pltpu.VMEM((PARTS, COEFS, CELLS), BF16),
        pltpu.VMEM((2 * MODES, COEFS), BF16),
        pltpu.VMEM((COEFS, 2 * MODES), BF16),
        pltpu.VMEM((2, MODES, LANES), F32),
        pltpu.VMEM(by_in.shape, BF16),
        pltpu.VMEM(by_in_t.shape, BF16),
        pltpu.VMEM(by_out.shape, BF16),
        pltpu.VMEM(by_out_t.shape, BF16),
        pltpu.VMEM((LANES, CELLS), BF16),
        pltpu.VMEM((LANES, CELLS), BF16),
        pltpu.VMEM((LANES, CELLS), BF16),
        pltpu.VMEM((LANES, CELLS), F32),
        pltpu.VMEM((PARTS * SHARE, 2 * MIX), BF16),
        pltpu.VMEM((PARTS, GROUPS, SHARE, 2 * MIX), BF16),
        pltpu.VMEM((PARTS, 2, MODES, MIX), F32),
        pltpu.VMEM((2, MODES, LANES), BF16),
        pltpu.VMEM((2, MODES, MIX), BF16),
        pltpu.VMEM((PARTS, GROUPS, SHARE, 2 * MIX), BF16),
        pltpu.VMEM((PARTS, GROUPS, SHARE, 2 * MIX), BF16),
        pltpu.VMEM((PARTS, COEFS, LANES), F32),
        pltpu.VMEM((4 * PARTS, SLABS, PIECE, LANES), BF16),
        pltpu.VMEM((4 * PARTS, SLABS, PIECE, LANES), BF16),
        pltpu.VMEM((LANES, LANES), BF16),
        pltpu.VMEM((LANES, LANES), BF16),
        pltpu.SemaphoreType.DMA((14,)),
        pltpu.SemaphoreType.DMA((2,)),
        pltpu.SemaphoreType.DMA((4 * PARTS,)),
        pltpu.SemaphoreType.DMA((4 * PARTS,)),
        pltpu.SemaphoreType.DMA((2,)),
        pltpu.SemaphoreType.DMA((2 * PARTS,)),
    ]
    act, fgrad, wgrad = pl.pallas_call(
        kernel,
        out_shape=(
            jax.ShapeDtypeStruct((LANES, CELLS), BF16),
            jax.ShapeDtypeStruct((LANES, CELLS), BF16),
            jax.ShapeDtypeStruct((PARTS * SHARE, 2 * MIX), F32),
        ),
        in_specs=[anywhere] * 13,
        out_specs=(anywhere, anywhere, vmem),
        scratch_shapes=scratch,
        compiler_params=pltpu.CompilerParams(
            collective_id=0, has_side_effects=True, vmem_limit_bytes=60 * 1024 * 1024
        ),
        cost_estimate=pl.CostEstimate(
            flops=3_600_000_000, bytes_accessed=10_000_000, transcendentals=524288
        ),
        name="fourier_layer",
    )(
        field.reshape(LANES, CELLS), out_grad.reshape(LANES, CELLS),
        spec_weight.reshape(PARTS * SHARE, 2 * MIX), skip_weight, skip_bias.reshape(1, C), *tables,
    )
    return (
        act.reshape(field.shape), fgrad.reshape(field.shape), wgrad.reshape(spec_weight.shape)
    )


def solution(mesh):
    in_specs = (
        P("dp", None, "mp", None),
        P("dp", "mp", None, None, None),
        P(),
        P(),
        P("dp", None, "mp", None),
    )
    out_specs = (
        P("dp", None, "mp", None),
        P("dp", None, "mp", None),
        P("dp", "mp", None, None, None),
    )
    return jax.shard_map(body, mesh=mesh, in_specs=in_specs, out_specs=out_specs, check_vma=False)
```

time: 103 us -> 93 us (0.903)
  local copies, waits for them, and re-layouts: 13.3 us -> 7.1 us
  Pallas kernels: 88.3 us -> 85 us
    unnamed x22 -> x4, local copies, waits for them, and re-layouts: 11.1 us -> 3.28 us
    pallas_call x1, Pallas kernels: 88.3 us -> 85 us  [body(): pl.pallas_call(kernel, out_shape=(jax.ShapeDtypeStruct((LANES, CELLS), BF...]
where the time goes in v1:
time: 93 us; the launch traced here: 92.8 us
  Pallas kernels  85 us (91%)
  local copies, waits for them, and re-layouts  7.1 us (8%)
    pallas_call x1, Pallas kernels, body(): pl.pallas_call(kernel, out_shape=(jax.ShapeDtypeStruct((LANES, CELLS), BF...  85 us
    unnamed x4, local copies, waits for them, and re-layouts  3.28 us
    reshape x1, local copies, waits for them, and re-layouts, body(): wgrad.reshape(spec_weight.shape)  1.96 us
    reshape x1, local copies, waits for them, and re-layouts, body(): spec_weight.reshape(PARTS * SHARE, 2 * MIX)  1.87 us

profile of v1, /device:TPU:1, one launch (start us, length us, event | category | flops | bytes accessed | tf_op | source)
XLA Modules:
  0.0 92.8 jit_solution(1182993056178290932)
XLA Ops:
  0.6 1.9 %reshape.29.weight_hbm = bf16[16,2048]{1,0:T(8,128)(2,1)} reshape(bf16[2,8,2,32,32]{4,3,2,1,0:T(8,128)(2,1)} %param.14) | data formatting | bytes 131072 | tf_op jit(solution)/shard_map/reshape | solution.py:487
  2.5 85.0 %fourier_layer.1 = (bf16[256,2048]{1,0:T(8,128)(2,1)}, bf16[256,2048]{1,0:T(8,128)(2,1)}, f32[16,2048]{1,0:T(8,128)}) custom-call(bf16[256,2048]{1,0:T(8,128)(2,1)} %bitcast.9, bf16[256,2048]{1,0:T(8,128)(2,1)} %bitcast.10, bf16[16,2048]{1,0:T(8,128)(2,1)} %reshape.29.weight_hbm, bf16[32,32]{1,0:T(8,128)(2,1)} %skip_hbm.1, f32[1,32]{1,0:T(1,128)} %bitcast.11, ...), custom_call_target="tpu_custom_call" | custom-call | flops 3600000000 | bytes 10000000 | tf_op jit(solution)/shard_map/fourier_layer/pallas_call | solution.py:468
  87.5 0.0 copy-start
  87.5 2.0 %reshape.33 = f32[2,8,2,32,32]{4,3,2,1,0:T(8,128)} reshape(f32[16,2048]{1,0:T(8,128)} %get-tuple-element.8) | data formatting | bytes 262144 | tf_op jit(solution)/shard_map/reshape | solution.py:490
  89.5 2.3 %copy.18 = bf16[1,32,8,2048]{3,2,1,0:T(8,128)(2,1)} copy(bf16[1,32,8,2048]{3,2,1,0:T(8,128)(2,1)} %bitcast.8) | data formatting | bytes 2097152
  91.8 0.0 copy-done
  91.8 1.0 %copy.19 = bf16[1,32,8,2048]{3,2,1,0:T(8,128)(2,1)} copy(bf16[1,32,8,2048]{3,2,1,0:T(8,128)(2,1)S(1)} %bitcast.7) | data formatting | bytes 2097152
Async XLA Ops:
  87.5 4.3 %copy-start = (bf16[256,2048]{1,0:T(8,128)(2,1)S(1)}, bf16[256,2048]{1,0:T(8,128)(2,1)}, u32[]{:S(2)}) copy-start(bf16[256,2048]{1,0:T(8,128)(2,1)} %get-tuple-element.7) | copy-start | bytes 3145732

commit v2 on v1

--- a/solution.py
+++ b/solution.py
@@ -23,6 +23,8 @@
 PARTS = 2
 PART = PAIRS // PARTS
 GROUPS = 16
+CHIPS = 8
+CORES = 2
 OWN = KX // GROUPS
 MODES = KX * PART
 LANES = C * ROWS
@@ -79,6 +81,15 @@
     return by_in, by_in.T.copy(), by_out, by_out.T.copy()
 
 
+def share_tables():
+    tile = (np.arange(C)[:, None] == np.arange(MIX) % C).astype(np_bf16)
+    out = np.arange(2 * PARTS * SHARE)
+    r, part, own, pair = out // (PARTS * SHARE), out // SHARE % PARTS, out // PART % OWN, out % PART
+    source = (own * PAIRS + part * PART + pair) * 2 + r
+    pick = (source[:, None] == np.arange(2 * PARTS * SHARE * C) // C).astype(np_bf16)
+    return tile, pick
+
+
 def regroup(first, second):
     upper = lax.broadcasted_iota(jnp.int32, first.shape, 0) < PART
     return (
@@ -97,13 +108,15 @@
 def kernel(
     field_hbm, cot_hbm, weight_hbm, skip_hbm, bias_hbm,
     grid_hbm, slab_hbm, back_hbm, row_hbm, e_in_hbm, e_in_t_hbm, e_out_hbm, e_out_t_hbm,
+    tile_hbm, pick_hbm,
     act_hbm, fgrad_hbm, wgrad_ref,
     field, cot, skip_v, bias_v, grid, slab, slab_b, rowt, e_in, e_in_t, e_out, e_out_t,
-    act, gpre, fgrad, lin, share, weight, u_rep, coef, gs, wg, wg_recv, acc, send, recv, mixk, mixk_t,
-    load_sem, store_sem, send_sem, recv_sem, gather_sem, reduce_sem,
+    act, gpre, fgrad, lin, share, tile, pick, weight, u_rep, coef, gs, wg, wg_recv, acc, send, recv, mixk, mixk_t,
+    load_sem, store_sem, send_sem, recv_sem, gather_sem, sibling_sem, reduce_sem,
 ):
     dp = lax.axis_index("dp")
     mp = lax.axis_index("mp")
+    chip, core = dp // CORES, lax.rem(dp, CORES)
 
     loads = [
         pltpu.make_async_copy(src, dst, load_sem.at[i])
@@ -112,7 +125,8 @@
                 (field_hbm, field), (grid_hbm.at[0], grid.at[0]), (grid_hbm.at[1], grid.at[1]),
                 (skip_hbm, skip_v), (bias_hbm, bias_v), (slab_hbm, slab), (row_hbm, rowt),
                 (e_in_hbm, e_in), (e_out_hbm, e_out), (back_hbm, slab_b), (cot_hbm, cot),
-                (e_in_t_hbm, e_in_t), (e_out_t_hbm, e_out_t), (weight_hbm, share),
+                (e_in_t_hbm, e_in_t), (e_out_t_hbm, e_out_t), (weight_hbm, share), (tile_hbm, tile),
+                (pick_hbm, pick),
             ]
         )
     ]
@@ -169,33 +183,67 @@
     def cells_of(i):
         return pl.ds(pl.multiple_of(i * CHUNK, CHUNK), CHUNK)
 
+    def push_weights(part):
+        def push(i, carry):
+            peer = lax.rem(dp + CORES * i, GROUPS)
+            pltpu.make_async_remote_copy(
+                src_ref=weight.at[part, chip, core],
+                dst_ref=weight.at[part, chip, core],
+                send_sem=gather_sem.at[part],
+                recv_sem=gather_sem.at[PARTS + part],
+                device_id={"dp": peer},
+                device_id_type=MESH,
+            ).start()
+            return carry
+
+        lax.fori_loop(1, CHIPS, push, 0)
+
+    def chips_block(part):
+        block = weight.at[part, pl.ds(0, CHIPS - 1), 0]
+        return block, block
+
+    def pass_weights(part):
+        pltpu.make_async_copy(*chips_block(part), gather_sem.at[PARTS + part]).wait()
+        pltpu.make_async_remote_copy(
+            src_ref=weight.at[part, :, core],
+            dst_ref=weight.at[part, :, core],
+            send_sem=sibling_sem.at[part],
+            recv_sem=sibling_sem.at[PARTS + part],
+            device_id={"dp": dp + 1 - 2 * core},
+            device_id_type=MESH,
+        ).start()
+
+    def half_block(part):
+        block = weight.at[part, :, 0]
+        return block, block
+
     loads[0].wait()
     loads[1].wait()
     outgoing(0, 0, dot(grid[0], field[...], NT))
+    for copy in loads[13:]:
+        copy.wait()
+    diagonal = (
+        lax.broadcasted_iota(jnp.int32, (LANES, MIX), 0) % C
+        == lax.broadcasted_iota(jnp.int32, (LANES, MIX), 1) // C
+    )
+    laid = jnp.zeros((2 * PARTS * SHARE, MIX), F32)
+    for n in range(0, PARTS * SHARE * 2 * C, LANES):
+        spread_rows = jnp.where(diagonal, dot(share[n : n + LANES], tile[...]), 0.0)
+        laid = laid + dot(pick[:, n : n + LANES], spread_rows.astype(BF16))
+    for part in range(PARTS):
+        for r in range(2):
+            first_row = (r * PARTS + part) * SHARE
+            weight[part, chip, core, :, r * MIX : (r + 1) * MIX] = laid[
+                first_row : first_row + SHARE
+            ].astype(BF16)
     pl.semaphore_wait(barrier, SLABS + GROUPS - 2)
+    push_weights(0)
     exchange(0, 0)
     loads[2].wait()
     outgoing(0, 1, dot(grid[1], field[...], NT))
     exchange(0, 1)
 
-    def push_weight(i, carry):
-        peer = lax.rem(dp + i, GROUPS)
-        pltpu.make_async_remote_copy(
-            src_ref=weight.at[:, dp],
-            dst_ref=weight.at[:, dp],
-            send_sem=gather_sem.at[0],
-            recv_sem=gather_sem.at[1],
-            device_id={"dp": peer},
-            device_id_type=MESH,
-        ).start()
-        return carry
-
-    for copy in loads[3:]:
-        copy.wait()
-    parted = regroup(share[:SHARE].astype(F32), share[SHARE:].astype(F32))
-    for part in range(PARTS):
-        weight[part, dp] = parted[part].astype(BF16)
-    lax.fori_loop(1, GROUPS, push_weight, 0)
+    push_weights(1)
 
     rep = (
         lax.broadcasted_iota(jnp.int32, (LANES, C), 0) // ROWS
@@ -206,6 +254,8 @@
         lax.broadcasted_iota(jnp.int32, (LANES, LANES), 0) % ROWS
         == lax.broadcasted_iota(jnp.int32, (LANES, LANES), 1) % ROWS
     )
+    for copy in loads[3:13]:
+        copy.wait()
     skip = skip_v[...]
     by_out = dot(dot(rep_b, skip, NT).astype(BF16), rep_b, NT)
     by_in = dot(dot(rep_b, skip).astype(BF16), rep_b, NT)
@@ -217,6 +267,7 @@
         lin[:, cells_of(i)] = dot(mixk[...], field[:, cells_of(i)]) + bias
         return carry
 
+    pass_weights(0)
     lax.fori_loop(0, CELLS // CHUNK, linear, 0)
 
     doubled = [
@@ -243,9 +294,9 @@
         return pl.ds(pl.multiple_of(i * STRIP, STRIP), STRIP)
 
     def weights_of(part, i, t):
-        owners = pl.ds(i * (STRIP // SHARE), STRIP // SHARE)
-        w0 = weight[part, owners, :, t : t + 128].astype(F32).reshape(STRIP, 128)
-        w1 = weight[part, owners, :, MIX + t : MIX + t + 128].astype(F32).reshape(STRIP, 128)
+        chips = pl.ds(i * (STRIP // SHARE // CORES), STRIP // SHARE // CORES)
+        w0 = weight[part, chips, :, :, t : t + 128].astype(F32).reshape(STRIP, 128)
+        w1 = weight[part, chips, :, :, MIX + t : MIX + t + 128].astype(F32).reshape(STRIP, 128)
         return w0, w1
 
     for part in range(PARTS):
@@ -256,9 +307,7 @@
                 u_rep[part, q, :, h * MIX // 2 : (h + 1) * MIX // 2] = dot(
                     coef[q, :, h * 128 : (h + 1) * 128], e_in[...]
                 )
-        if part == 0:
-            gathered = weight.at[:, pl.ds(0, GROUPS - 1)]
-            pltpu.make_async_copy(gathered, gathered, gather_sem.at[1]).wait()
+        pltpu.make_async_copy(*half_block(part), sibling_sem.at[PARTS + part]).wait()
 
         def mix(i, carry):
             rows = strip_of(i)
@@ -283,6 +332,8 @@
             ),
         )
         exchange(1, part)
+        if part == 0:
+            pass_weights(1)
 
     back = arrived(1, 0).T
 
@@ -412,7 +463,9 @@
     for slot in range(4 * PARTS):
         block = send.at[slot, pl.ds(0, SLABS - 1)]
         pltpu.make_async_copy(block, block, send_sem.at[slot]).wait()
-    pltpu.make_async_copy(gathered, gathered, gather_sem.at[0]).wait()
+    for part in range(PARTS):
+        pltpu.make_async_copy(*chips_block(part), gather_sem.at[part]).wait()
+        pltpu.make_async_copy(*half_block(part), sibling_sem.at[part]).wait()
     for part in range(PARTS):
         sent = wg.at[part, pl.ds(0, GROUPS - 1)]
         pltpu.make_async_copy(sent, sent, reduce_sem.at[part]).wait()
@@ -420,12 +473,34 @@
     store_grad.wait()
 
 
+def hand_out(act_in, fgrad_in, act_out, fgrad_out, act, fgrad, in_sem, out_sem):
+    rows = LANES // 4
+    blocks = [
+        (k, n // rows, src.at[pl.ds(n, rows)], mid.at[pl.ds(n, rows)], dst.at[pl.ds(n, rows)])
+        for k, (src, mid, dst) in enumerate([(act_in, act, act_out), (fgrad_in, fgrad, fgrad_out)])
+        for n in range(0, LANES, rows)
+    ]
+    loads = [pltpu.make_async_copy(src, mid, in_sem.at[k, n]) for k, n, src, mid, _ in blocks]
+    stores = [pltpu.make_async_copy(mid, dst, out_sem.at[k, n]) for k, n, _, mid, dst in blocks]
+    for load in loads:
+        load.start()
+    for load, store in zip(loads, stores):
+        load.wait()
+        store.start()
+    for store in stores:
+        store.wait()
+
+
 def body(field, spec_weight, skip_weight, skip_bias, out_grad):
     slab = slab_table()
     by_in, by_in_t, by_out, by_out_t = spread_tables()
+    tile, pick = share_tables()
     tables = [
         jnp.asarray(t)
-        for t in (grid_table(), slab, slab.T.copy(), row_tables(), by_in, by_in_t, by_out, by_out_t)
+        for t in (
+            grid_table(), slab, slab.T.copy(), row_tables(), by_in, by_in_t, by_out, by_out_t,
+            tile, pick,
+        )
     ]
     anywhere = pl.BlockSpec(memory_space=pl.ANY)
     vmem = pl.BlockSpec(memory_space=pltpu.VMEM)
@@ -446,8 +521,10 @@
         pltpu.VMEM((LANES, CELLS), BF16),
         pltpu.VMEM((LANES, CELLS), BF16),
         pltpu.VMEM((LANES, CELLS), F32),
-        pltpu.VMEM((PARTS * SHARE, 2 * MIX), BF16),
-        pltpu.VMEM((PARTS, GROUPS, SHARE, 2 * MIX), BF16),
+        pltpu.VMEM((PARTS * SHARE * 2 * C, C), BF16),
+        pltpu.VMEM(tile.shape, BF16),
+        pltpu.VMEM(pick.shape, BF16),
+        pltpu.VMEM((PARTS, CHIPS, CORES, SHARE, 2 * MIX), BF16),
         pltpu.VMEM((PARTS, 2, MODES, MIX), F32),
         pltpu.VMEM((2, MODES, LANES), BF16),
         pltpu.VMEM((2, MODES, MIX), BF16),
@@ -458,11 +535,12 @@
         pltpu.VMEM((4 * PARTS, SLABS, PIECE, LANES), BF16),
         pltpu.VMEM((LANES, LANES), BF16),
         pltpu.VMEM((LANES, LANES), BF16),
-        pltpu.SemaphoreType.DMA((14,)),
+        pltpu.SemaphoreType.DMA((16,)),
         pltpu.SemaphoreType.DMA((2,)),
         pltpu.SemaphoreType.DMA((4 * PARTS,)),
         pltpu.SemaphoreType.DMA((4 * PARTS,)),
-        pltpu.SemaphoreType.DMA((2,)),
+        pltpu.SemaphoreType.DMA((2 * PARTS,)),
+        pltpu.SemaphoreType.DMA((2 * PARTS,)),
         pltpu.SemaphoreType.DMA((2 * PARTS,)),
     ]
     act, fgrad, wgrad = pl.pallas_call(
@@ -472,7 +550,7 @@
             jax.ShapeDtypeStruct((LANES, CELLS), BF16),
             jax.ShapeDtypeStruct((PARTS * SHARE, 2 * MIX), F32),
         ),
-        in_specs=[anywhere] * 13,
+        in_specs=[anywhere] * 15,
         out_specs=(anywhere, anywhere, vmem),
         scratch_shapes=scratch,
         compiler_params=pltpu.CompilerParams(
@@ -484,8 +562,22 @@
         name="fourier_layer",
     )(
         field.reshape(LANES, CELLS), out_grad.reshape(LANES, CELLS),
-        spec_weight.reshape(PARTS * SHARE, 2 * MIX), skip_weight, skip_bias.reshape(1, C), *tables,
-    )
+        spec_weight.reshape(PARTS * SHARE * 2 * C, C), skip_weight, skip_bias.reshape(1, C), *tables,
+    )
+    act, fgrad = pl.pallas_call(
+        hand_out,
+        out_shape=(jax.ShapeDtypeStruct((LANES, CELLS), BF16),) * 2,
+        in_specs=[anywhere] * 2,
+        out_specs=(anywhere, anywhere),
+        scratch_shapes=[
+            pltpu.VMEM((LANES, CELLS), BF16),
+            pltpu.VMEM((LANES, CELLS), BF16),
+            pltpu.SemaphoreType.DMA((2, 4)),
+            pltpu.SemaphoreType.DMA((2, 4)),
+        ],
+        compiler_params=pltpu.CompilerParams(vmem_limit_bytes=60 * 1024 * 1024),
+        name="hand_out",
+    )(act, fgrad)
     return (
         act.reshape(field.shape), fgrad.reshape(field.shape), wgrad.reshape(spec_weight.shape)
     )

time: 93 us -> 79.7 us (0.86)
  Pallas kernels: 85 us -> 77.6 us
  local copies, waits for them, and re-layouts: 7.1 us -> 0.97 us
    pallas_call x1, Pallas kernels: 85 us -> 75.2 us  [body(): pl.pallas_call(kernel, out_shape=(jax.ShapeDtypeStruct((LANES, CELLS), BF...]
    unnamed x4 -> x2, local copies, waits for them, and re-layouts: 3.28 us -> 0.01 us
    pallas_call x0 -> x1, Pallas kernels: none -> 2.43 us  [body(): pl.pallas_call(hand_out, out_shape=(jax.ShapeDtypeStruct((LANES, CELLS),...]
    reshape x1 -> x0, local copies, waits for them, and re-layouts: 1.87 us -> none  [body(): spec_weight.reshape(PARTS * SHARE, 2 * MIX)]
    reshape x1, local copies, waits for them, and re-layouts: 1.96 us -> 0.97 us  [body(): wgrad.reshape(spec_weight.shape)]
where the time goes in v2:
time: 79.7 us; the launch traced here: 79.3 us
  Pallas kernels  77.6 us (97%)
  local copies, waits for them, and re-layouts  0.97 us (1%)
    pallas_call x1, Pallas kernels, body(): pl.pallas_call(kernel, out_shape=(jax.ShapeDtypeStruct((LANES, CELLS), BF...  75.2 us
    pallas_call x1, Pallas kernels, body(): pl.pallas_call(hand_out, out_shape=(jax.ShapeDtypeStruct((LANES, CELLS),...  2.43 us

profile of v2, /device:TPU:1, one launch (start us, length us, event | category | flops | bytes accessed | tf_op | source)
XLA Modules:
  0.0 79.3 jit_solution(3602819327506018929)
XLA Ops:
  0.6 75.2 %fourier_layer.1 = (bf16[256,2048]{1,0:T(8,128)(2,1)}, bf16[256,2048]{1,0:T(8,128)(2,1)}, f32[16,2048]{1,0:T(8,128)}) custom-call(bf16[256,2048]{1,0:T(8,128)(2,1)} %bitcast.6, bf16[256,2048]{1,0:T(8,128)(2,1)} %bitcast.7, bf16[1024,32]{1,0:T(8,128)(2,1)} %bitcast.10, bf16[32,32]{1,0:T(8,128)(2,1)} %skip_hbm.1, f32[1,32]{1,0:T(1,128)} %bitcast.11, ...), custom_call_target="tpu_custom_call" | custom-call | flops 3600000000 | bytes 10000000 | tf_op jit(solution)/shard_map/fourier_layer/pallas_call | solution.py:546
  75.8 0.0 copy-start
  75.8 2.4 %hand_out.1 = (bf16[256,2048]{1,0:T(8,128)(2,1)}, bf16[256,2048]{1,0:T(8,128)(2,1)}) custom-call(bf16[256,2048]{1,0:T(8,128)(2,1)} %get-tuple-element.8.act_in, bf16[256,2048]{1,0:T(8,128)(2,1)} %get-tuple-element.9.fgrad_in), custom_call_target="tpu_custom_call" | custom-call | tf_op jit(solution)/shard_map/hand_out/pallas_call | solution.py:567
  78.3 0.0 copy-done
  78.3 1.0 %reshape.33 = f32[2,8,2,32,32]{4,3,2,1,0:T(8,128)} reshape(f32[16,2048]{1,0:T(8,128)S(1)} %copy-done) | data formatting | bytes 262144 | tf_op jit(solution)/shard_map/reshape | solution.py:582
Async XLA Ops:
  75.8 2.5 %copy-start = (f32[16,2048]{1,0:T(8,128)S(1)}, f32[16,2048]{1,0:T(8,128)}, u32[]{:S(2)}) copy-start(f32[16,2048]{1,0:T(8,128)} %get-tuple-element.12) | copy-start | bytes 393220

commit v3 on v2

--- a/solution.py
+++ b/solution.py
@@ -25,6 +25,7 @@
 GROUPS = 16
 CHIPS = 8
 CORES = 2
+FAR = 8
 OWN = KX // GROUPS
 MODES = KX * PART
 LANES = C * ROWS
@@ -32,8 +33,9 @@
 PIECE = 2 * PART
 SHARE = OWN * PART
 MIX = C * C
-CHUNK = 512
+CHUNK = 1024
 STRIP = 32
+PIECES_OUT = 4
 MESH = pl.DeviceIdType.MESH
 F32 = jnp.float32
 BF16 = jnp.bfloat16
@@ -81,15 +83,6 @@
     return by_in, by_in.T.copy(), by_out, by_out.T.copy()
 
 
-def share_tables():
-    tile = (np.arange(C)[:, None] == np.arange(MIX) % C).astype(np_bf16)
-    out = np.arange(2 * PARTS * SHARE)
-    r, part, own, pair = out // (PARTS * SHARE), out // SHARE % PARTS, out // PART % OWN, out % PART
-    source = (own * PAIRS + part * PART + pair) * 2 + r
-    pick = (source[:, None] == np.arange(2 * PARTS * SHARE * C) // C).astype(np_bf16)
-    return tile, pick
-
-
 def regroup(first, second):
     upper = lax.broadcasted_iota(jnp.int32, first.shape, 0) < PART
     return (
@@ -108,10 +101,9 @@
 def kernel(
     field_hbm, cot_hbm, weight_hbm, skip_hbm, bias_hbm,
     grid_hbm, slab_hbm, back_hbm, row_hbm, e_in_hbm, e_in_t_hbm, e_out_hbm, e_out_t_hbm,
-    tile_hbm, pick_hbm,
-    act_hbm, fgrad_hbm, wgrad_ref,
+    act_hbm, fgrad_hbm, wgrad_hbm,
     field, cot, skip_v, bias_v, grid, slab, slab_b, rowt, e_in, e_in_t, e_out, e_out_t,
-    act, gpre, fgrad, lin, share, tile, pick, weight, u_rep, coef, gs, wg, wg_recv, acc, send, recv, mixk, mixk_t,
+    act, gpre, fgrad, wgrad, lin, share, share_wide, laid, weight, u_rep, coef, gs, wg, wg_recv, acc, send, recv, mixk, mixk_t,
     load_sem, store_sem, send_sem, recv_sem, gather_sem, sibling_sem, reduce_sem,
 ):
     dp = lax.axis_index("dp")
@@ -125,12 +117,11 @@
                 (field_hbm, field), (grid_hbm.at[0], grid.at[0]), (grid_hbm.at[1], grid.at[1]),
                 (skip_hbm, skip_v), (bias_hbm, bias_v), (slab_hbm, slab), (row_hbm, rowt),
                 (e_in_hbm, e_in), (e_out_hbm, e_out), (back_hbm, slab_b), (cot_hbm, cot),
-                (e_in_t_hbm, e_in_t), (e_out_t_hbm, e_out_t), (weight_hbm, share), (tile_hbm, tile),
-                (pick_hbm, pick),
+                (e_in_t_hbm, e_in_t), (e_out_t_hbm, e_out_t), (weight_hbm, share),
             ]
         )
     ]
-    for copy in loads:
+    for copy in loads[:2] + loads[13:]:
         copy.start()
 
     barrier = pltpu.get_barrier_semaphore()
@@ -151,12 +142,9 @@
     def exchange(phase, part):
         slot = phase * PARTS + part
 
-        def push(i, carry):
-            turn = SLABS - i
-            hop = turn // 2
-            shift = (hop + 1) // 2 * (2 * lax.rem(hop, 2) - 1)
+        def push(shift, flip):
             z = lax.rem(mp + shift + SLABS, SLABS // 2)
-            y = lax.rem(mp // (SLABS // 2) + turn, 2)
+            y = lax.rem(mp // (SLABS // 2) + flip, 2)
             peer = y * (SLABS // 2) + z
             pltpu.make_async_remote_copy(
                 src_ref=send.at[slot, peer],
@@ -166,9 +154,19 @@
                 device_id={"mp": peer},
                 device_id_type=MESH,
             ).start()
+
+        def push_at(n, carry):
+            hop = FAR - n
+            far = hop + 2
+            pl.when(far <= FAR)(lambda: push(far, 0))
+            pl.when(far < FAR)(lambda: push(-far, 0))
+            push(hop, 1)
+            pl.when((hop > 0) & (hop < FAR))(lambda: push(-hop, 1))
             return carry
 
-        lax.fori_loop(1, SLABS, push, 0)
+        lax.fori_loop(0, FAR + 1, push_at, 0)
+        push(1, 0)
+        push(-1, 0)
         recv[slot, mp] = send[slot, mp]
 
     def arrived(phase, part):
@@ -182,6 +180,12 @@
 
     def cells_of(i):
         return pl.ds(pl.multiple_of(i * CHUNK, CHUNK), CHUNK)
+
+    for copy in loads[2:13]:
+        copy.start()
+
+    def rows_of(r, c):
+        return pl.ds(r * C + c, PARTS * SHARE, stride=2 * C)
 
     def push_weights(part):
         def push(i, carry):
@@ -222,20 +226,13 @@
     outgoing(0, 0, dot(grid[0], field[...], NT))
     for copy in loads[13:]:
         copy.wait()
-    diagonal = (
-        lax.broadcasted_iota(jnp.int32, (LANES, MIX), 0) % C
-        == lax.broadcasted_iota(jnp.int32, (LANES, MIX), 1) // C
-    )
-    laid = jnp.zeros((2 * PARTS * SHARE, MIX), F32)
-    for n in range(0, PARTS * SHARE * 2 * C, LANES):
-        spread_rows = jnp.where(diagonal, dot(share[n : n + LANES], tile[...]), 0.0)
-        laid = laid + dot(pick[:, n : n + LANES], spread_rows.astype(BF16))
-    for part in range(PARTS):
-        for r in range(2):
-            first_row = (r * PARTS + part) * SHARE
-            weight[part, chip, core, :, r * MIX : (r + 1) * MIX] = laid[
-                first_row : first_row + SHARE
-            ].astype(BF16)
+    share_wide[...] = share[...].astype(F32)
+    for r in range(2):
+        for c in range(C):
+            laid[r, :, c * C : (c + 1) * C] = share_wide[rows_of(r, c), :]
+        parted = regroup(laid[r, :SHARE], laid[r, SHARE:])
+        for part in range(PARTS):
+            weight[part, chip, core, :, r * MIX : (r + 1) * MIX] = parted[part].astype(BF16)
     pl.semaphore_wait(barrier, SLABS + GROUPS - 2)
     push_weights(0)
     exchange(0, 0)
@@ -343,7 +340,6 @@
 
     lax.fori_loop(0, CELLS // CHUNK, spread, 0)
     back_last = arrived(1, 1).T
-    acc[...] = jnp.zeros((PARTS, COEFS, LANES), F32)
     root = math.sqrt(2.0 / math.pi)
     cube = 0.044715
 
@@ -351,20 +347,17 @@
         cells = cells_of(i)
         pre = dot(back_last, grid[1, :, cells]) + lin[:, cells]
         square = pre * pre
-        bent = jnp.tanh(pre * (root + (root * cube) * square))
-        half = 0.5 * pre
-        upper = 0.5 + 0.5 * bent
-        act[:, cells] = (pre * upper).astype(BF16)
-        slope = upper + half * (1.0 - bent * bent) * (root + (3.0 * root * cube) * square)
+        upper = 0.5 + 0.5 * jnp.tanh(pre * (root + (root * cube) * square))
+        out = pre * upper
+        act[:, cells] = out.astype(BF16)
+        slope = upper + out * (1.0 - upper) * (2.0 * root + (6.0 * root * cube) * square)
         grad = (cot[:, cells].astype(F32) * slope).astype(BF16)
         gpre[:, cells] = grad
-        acc[0] += dot(grid[0, :, cells], grad, NT)
-        acc[1] += dot(grid[1, :, cells], grad, NT)
         return carry
 
     lax.fori_loop(0, CELLS // CHUNK, activate, 0)
     for part in range(PARTS):
-        outgoing(2, part, acc[part])
+        outgoing(2, part, dot(grid[part], gpre[...], NT))
         exchange(2, part)
     store_act = pltpu.make_async_copy(act, act_hbm, store_sem.at[0])
     store_act.start()
@@ -439,14 +432,15 @@
     lax.fori_loop(0, CELLS // CHUNK, spread_back, 0)
     grad_back_last = arrived(3, 1).T
 
-    def finish(i, carry):
-        cells = cells_of(i)
+    stores_grad = []
+    for n in range(0, CELLS, CHUNK):
+        cells = pl.ds(n, CHUNK)
         fgrad[:, cells] = (dot(grad_back_last, grid[1, :, cells]) + lin[:, cells]).astype(BF16)
-        return carry
-
-    lax.fori_loop(0, CELLS // CHUNK, finish, 0)
-    store_grad = pltpu.make_async_copy(fgrad, fgrad_hbm, store_sem.at[1])
-    store_grad.start()
+        store = pltpu.make_async_copy(
+            fgrad.at[:, cells], fgrad_hbm.at[:, cells], store_sem.at[3 + n // CHUNK]
+        )
+        store.start()
+        stores_grad.append(store)
 
     totals = []
     for part in range(PARTS):
@@ -457,8 +451,13 @@
             total = total + wg_recv[part, s].astype(F32)
         totals.append(total)
     whole = regroup(*totals)
-    for part in range(PARTS):
-        wgrad_ref[part * SHARE : (part + 1) * SHARE] = whole[part]
+    for r in range(2):
+        for part in range(PARTS):
+            laid[r, part * SHARE : (part + 1) * SHARE] = whole[part][:, r * MIX : (r + 1) * MIX]
+        for c in range(C):
+            wgrad[rows_of(r, c), :] = laid[r, :, c * C : (c + 1) * C]
+    store_wgrad = pltpu.make_async_copy(wgrad, wgrad_hbm, store_sem.at[2])
+    store_wgrad.start()
 
     for slot in range(4 * PARTS):
         block = send.at[slot, pl.ds(0, SLABS - 1)]
@@ -470,16 +469,22 @@
         sent = wg.at[part, pl.ds(0, GROUPS - 1)]
         pltpu.make_async_copy(sent, sent, reduce_sem.at[part]).wait()
     store_act.wait()
-    store_grad.wait()
-
-
-def hand_out(act_in, fgrad_in, act_out, fgrad_out, act, fgrad, in_sem, out_sem):
-    rows = LANES // 4
-    blocks = [
-        (k, n // rows, src.at[pl.ds(n, rows)], mid.at[pl.ds(n, rows)], dst.at[pl.ds(n, rows)])
-        for k, (src, mid, dst) in enumerate([(act_in, act, act_out), (fgrad_in, fgrad, fgrad_out)])
-        for n in range(0, LANES, rows)
-    ]
+    store_wgrad.wait()
+    for copy in stores_grad:
+        copy.wait()
+
+
+def hand_out(
+    act_in, fgrad_in, wgrad_in, act_out, fgrad_out, wgrad_out, act, fgrad, wgrad, in_sem, out_sem
+):
+    blocks = []
+    for k, (src, mid, dst) in enumerate(
+        [(act_in, act, act_out), (fgrad_in, fgrad, fgrad_out), (wgrad_in, wgrad, wgrad_out)]
+    ):
+        rows = src.shape[0] // PIECES_OUT
+        for n in range(PIECES_OUT):
+            block = pl.ds(n * rows, rows)
+            blocks.append((k, n, src.at[block], mid.at[block], dst.at[block]))
     loads = [pltpu.make_async_copy(src, mid, in_sem.at[k, n]) for k, n, src, mid, _ in blocks]
     stores = [pltpu.make_async_copy(mid, dst, out_sem.at[k, n]) for k, n, _, mid, dst in blocks]
     for load in loads:
@@ -494,16 +499,13 @@
 def body(field, spec_weight, skip_weight, skip_bias, out_grad):
     slab = slab_table()
     by_in, by_in_t, by_out, by_out_t = spread_tables()
-    tile, pick = share_tables()
     tables = [
         jnp.asarray(t)
         for t in (
             grid_table(), slab, slab.T.copy(), row_tables(), by_in, by_in_t, by_out, by_out_t,
-            tile, pick,
         )
     ]
     anywhere = pl.BlockSpec(memory_space=pl.ANY)
-    vmem = pl.BlockSpec(memory_space=pltpu.VMEM)
     scratch = [
         pltpu.VMEM((LANES, CELLS), BF16),
         pltpu.VMEM((LANES, CELLS), BF16),
@@ -520,10 +522,11 @@
         pltpu.VMEM((LANES, CELLS), BF16),
         pltpu.VMEM((LANES, CELLS), BF16),
         pltpu.VMEM((LANES, CELLS), BF16),
+        pltpu.VMEM((PARTS * SHARE * 2 * C, C), F32),
         pltpu.VMEM((LANES, CELLS), F32),
         pltpu.VMEM((PARTS * SHARE * 2 * C, C), BF16),
-        pltpu.VMEM(tile.shape, BF16),
-        pltpu.VMEM(pick.shape, BF16),
+        pltpu.VMEM((PARTS * SHARE * 2 * C, C), F32),
+        pltpu.VMEM((2, PARTS * SHARE, MIX), F32),
         pltpu.VMEM((PARTS, CHIPS, CORES, SHARE, 2 * MIX), BF16),
         pltpu.VMEM((PARTS, 2, MODES, MIX), F32),
         pltpu.VMEM((2, MODES, LANES), BF16),
@@ -535,8 +538,8 @@
         pltpu.VMEM((4 * PARTS, SLABS, PIECE, LANES), BF16),
         pltpu.VMEM((LANES, LANES), BF16),
         pltpu.VMEM((LANES, LANES), BF16),
-        pltpu.SemaphoreType.DMA((16,)),
-        pltpu.SemaphoreType.DMA((2,)),
+        pltpu.SemaphoreType.DMA((14,)),
+        pltpu.SemaphoreType.DMA((3 + CELLS // CHUNK,)),
         pltpu.SemaphoreType.DMA((4 * PARTS,)),
         pltpu.SemaphoreType.DMA((4 * PARTS,)),
         pltpu.SemaphoreType.DMA((2 * PARTS,)),
@@ -548,10 +551,10 @@
         out_shape=(
             jax.ShapeDtypeStruct((LANES, CELLS), BF16),
             jax.ShapeDtypeStruct((LANES, CELLS), BF16),
-            jax.ShapeDtypeStruct((PARTS * SHARE, 2 * MIX), F32),
+            jax.ShapeDtypeStruct((PARTS * SHARE * 2 * C, C), F32),
         ),
-        in_specs=[anywhere] * 15,
-        out_specs=(anywhere, anywhere, vmem),
+        in_specs=[anywhere] * 13,
+        out_specs=(anywhere,) * 3,
         scratch_shapes=scratch,
         compiler_params=pltpu.CompilerParams(
             collective_id=0, has_side_effects=True, vmem_limit_bytes=60 * 1024 * 1024
@@ -564,20 +567,21 @@
         field.reshape(LANES, CELLS), out_grad.reshape(LANES, CELLS),
         spec_weight.reshape(PARTS * SHARE * 2 * C, C), skip_weight, skip_bias.reshape(1, C), *tables,
     )
-    act, fgrad = pl.pallas_call(
+    results = (act, fgrad, wgrad)
+    shapes = [(r.shape, r.dtype) for r in results]
+    act, fgrad, wgrad = pl.pallas_call(
         hand_out,
-        out_shape=(jax.ShapeDtypeStruct((LANES, CELLS), BF16),) * 2,
-        in_specs=[anywhere] * 2,
-        out_specs=(anywhere, anywhere),
+        out_shape=tuple(jax.ShapeDtypeStruct(*shape) for shape in shapes),
+        in_specs=[anywhere] * 3,
+        out_specs=(anywhere,) * 3,
         scratch_shapes=[
-            pltpu.VMEM((LANES, CELLS), BF16),
-            pltpu.VMEM((LANES, CELLS), BF16),
-            pltpu.SemaphoreType.DMA((2, 4)),
-            pltpu.SemaphoreType.DMA((2, 4)),
+            *(pltpu.VMEM(*shape) for shape in shapes),
+            pltpu.SemaphoreType.DMA((3, PIECES_OUT)),
+            pltpu.SemaphoreType.DMA((3, PIECES_OUT)),
         ],
         compiler_params=pltpu.CompilerParams(vmem_limit_bytes=60 * 1024 * 1024),
         name="hand_out",
-    )(act, fgrad)
+    )(*results)
     return (
         act.reshape(field.shape), fgrad.reshape(field.shape), wgrad.reshape(spec_weight.shape)
     )

time: 79.7 us -> 77.9 us (0.977)
  local copies, waits for them, and re-layouts: 0.97 us -> 0 us
    reshape x1 -> x0, local copies, waits for them, and re-layouts: 0.97 us -> none  [body(): wgrad.reshape(spec_weight.shape)]
where the time goes in v3:
time: 77.9 us; the launch traced here: 77.7 us
  Pallas kernels  77 us (99%)
    pallas_call x1, Pallas kernels, body(): pl.pallas_call(kernel, out_shape=(jax.ShapeDtypeStruct((LANES, CELLS), BF...  74.4 us
    pallas_call x1, Pallas kernels, body(): pl.pallas_call(hand_out, out_shape=tuple((jax.ShapeDtypeStruct(*shape) fo...  2.63 us

profile of v3, /device:TPU:1, one launch (start us, length us, event | category | flops | bytes accessed | tf_op | source)
XLA Modules:
  0.0 77.7 jit_solution(3218883642476177093)
XLA Ops:
  0.6 74.4 %fourier_layer.1 = (bf16[256,2048]{1,0:T(8,128)(2,1)}, bf16[256,2048]{1,0:T(8,128)(2,1)}, f32[1024,32]{1,0:T(8,128)}) custom-call(bf16[256,2048]{1,0:T(8,128)(2,1)} %bitcast.7, bf16[256,2048]{1,0:T(8,128)(2,1)} %bitcast.8, bf16[1024,32]{1,0:T(8,128)(2,1)} %bitcast.12, bf16[32,32]{1,0:T(8,128)(2,1)} %skip_hbm.1, f32[1,32]{1,0:T(1,128)} %bitcast.13, ...), custom_call_target="tpu_custom_call" | custom-call | flops 3600000000 | bytes 10000000 | tf_op jit(solution)/shard_map/fourier_layer/pallas_call | solution.py:549
  75.1 2.6 %hand_out.1 = (bf16[256,2048]{1,0:T(8,128)(2,1)}, bf16[256,2048]{1,0:T(8,128)(2,1)}, f32[1024,32]{1,0:T(8,128)}) custom-call(bf16[256,2048]{1,0:T(8,128)(2,1)} %get-tuple-element.9.act_in, bf16[256,2048]{1,0:T(8,128)(2,1)} %get-tuple-element.10.fgrad_in, f32[1024,32]{1,0:T(8,128)} %get-tuple-element.11.wgrad_in), custom_call_target="tpu_custom_call" | custom-call | tf_op jit(solution)/shard_map/hand_out/pallas_call | solution.py:572

commit v4 on v3

--- a/solution.py
+++ b/solution.py
@@ -25,7 +25,10 @@
 GROUPS = 16
 CHIPS = 8
 CORES = 2
-FAR = 8
+WAYS = sorted(
+    ((z, y) for z in range(-7, 9) for y in (0, 1) if (z, y) != (0, 0)),
+    key=lambda way: (-abs(way[0]) - 2 * way[1], -abs(way[0]), way[0] < 0),
+)
 OWN = KX // GROUPS
 MODES = KX * PART
 LANES = C * ROWS
@@ -142,7 +145,7 @@
     def exchange(phase, part):
         slot = phase * PARTS + part
 
-        def push(shift, flip):
+        for shift, flip in WAYS:
             z = lax.rem(mp + shift + SLABS, SLABS // 2)
             y = lax.rem(mp // (SLABS // 2) + flip, 2)
             peer = y * (SLABS // 2) + z
@@ -155,18 +158,6 @@
                 device_id_type=MESH,
             ).start()
 
-        def push_at(n, carry):
-            hop = FAR - n
-            far = hop + 2
-            pl.when(far <= FAR)(lambda: push(far, 0))
-            pl.when(far < FAR)(lambda: push(-far, 0))
-            push(hop, 1)
-            pl.when((hop > 0) & (hop < FAR))(lambda: push(-hop, 1))
-            return carry
-
-        lax.fori_loop(0, FAR + 1, push_at, 0)
-        push(1, 0)
-        push(-1, 0)
         recv[slot, mp] = send[slot, mp]
 
     def arrived(phase, part):

time: 77.9 us -> 77.3 us (level)
  no operation moved by 1% of the time
where the time goes in v4:
time: 77.3 us; the launch traced here: 77.2 us
  Pallas kernels  76.5 us (99%)
    pallas_call x1, Pallas kernels, body(): pl.pallas_call(kernel, out_shape=(jax.ShapeDtypeStruct((LANES, CELLS), BF...  73.9 us
    pallas_call x1, Pallas kernels, body(): pl.pallas_call(hand_out, out_shape=tuple((jax.ShapeDtypeStruct(*shape) fo...  2.63 us

profile of v4, /device:TPU:1, one launch (start us, length us, event | category | flops | bytes accessed | tf_op | source)
XLA Modules:
  0.0 77.2 jit_solution(10873676330208358962)
XLA Ops:
  0.6 73.9 %fourier_layer.1 = (bf16[256,2048]{1,0:T(8,128)(2,1)}, bf16[256,2048]{1,0:T(8,128)(2,1)}, f32[1024,32]{1,0:T(8,128)}) custom-call(bf16[256,2048]{1,0:T(8,128)(2,1)} %bitcast.7, bf16[256,2048]{1,0:T(8,128)(2,1)} %bitcast.8, bf16[1024,32]{1,0:T(8,128)(2,1)} %bitcast.12, bf16[32,32]{1,0:T(8,128)(2,1)} %skip_hbm.1, f32[1,32]{1,0:T(1,128)} %bitcast.13, ...), custom_call_target="tpu_custom_call" | custom-call | flops 3600000000 | bytes 10000000 | tf_op jit(solution)/shard_map/fourier_layer/pallas_call | solution.py:540
  74.5 2.6 %hand_out.1 = (bf16[256,2048]{1,0:T(8,128)(2,1)}, bf16[256,2048]{1,0:T(8,128)(2,1)}, f32[1024,32]{1,0:T(8,128)}) custom-call(bf16[256,2048]{1,0:T(8,128)(2,1)} %get-tuple-element.9.act_in, bf16[256,2048]{1,0:T(8,128)(2,1)} %get-tuple-element.10.fgrad_in, f32[1024,32]{1,0:T(8,128)} %get-tuple-element.11.wgrad_in), custom_call_target="tpu_custom_call" | custom-call | tf_op jit(solution)/shard_map/hand_out/pallas_call | solution.py:563
